TPU v7x, 32 devices: a whole 2x2x4 slice. The times are simulated.
32 devices in a mesh: groups: 2 (over y), ctx: 8 (over z, x), head: 2 (over core).
Axes of the slice: x: 2, y: 2, z: 4, core: 2. Of those that a mesh axis runs over, the one named last changes fastest.
Arguments:
- query_latent: bfloat16 [16, 64, 512], P(('groups', 'ctx'), 'head'), parts along dimension 0, may hold values from -16 to 16
- query_rope: bfloat16 [16, 64, 64], P(('groups', 'ctx'), 'head'), parts along dimension 0, may hold values from -6 to 6
- cache_latent: bfloat16 [4096, 512], P(('groups', 'ctx')), parts along dimension 0, may hold values from -4 to 4
- cache_rope: bfloat16 [4096, 64], P(('groups', 'ctx')), parts along dimension 0, may hold values from -6 to 6
- value_up: bfloat16 [64, 512, 128], P('head', 'ctx'), may hold values from -0.25 to 0.25
- out_proj: bfloat16 [128, 64, 7168], P('ctx', 'head'), may hold values from -0.25 to 0.25
Outputs:
- attended: bfloat16 [16, 7168], P(('groups', 'ctx'), 'head'), parts along dimension 0
There are 2 independent parts, one for each index of `groups`. A program takes and returns all parts, laid end to end along the dimension named above; an argument that names none is the same for every part. Nothing has to cross between parts.
All inputs are finite; a program needn't handle non-finite values.
Results may differ from a plain program's by a relative error of at most 0.0075.
Values may be sent and summed in bfloat16 or wider, within the bound.
A program may use at most 64 MiB of HBM per device.

v0:
```python
import jax
import jax.numpy as jnp
from jax import lax
from jax.sharding import PartitionSpec as P

ROPE = 64
NOPE = 128


def per_device(query_latent, query_rope, cache_latent, cache_rope, value_up, out_proj):
    score_scale = (NOPE + ROPE) ** (-0.5)
    rows_here, heads_here, latent_width = query_latent.shape
    rotary_width = query_rope.shape[2]
    latent_share, value_width = (value_up.shape[1], value_up.shape[2])
    column_share = out_proj.shape[0]
    per_block = min(8, heads_here)
    block_count = heads_here // per_block
    latent_blocks = jnp.transpose(
        query_latent.reshape(rows_here, block_count, per_block, latent_width), (1, 0, 2, 3)
    )
    rotary_blocks = jnp.transpose(
        query_rope.reshape(rows_here, block_count, per_block, rotary_width), (1, 0, 2, 3)
    )
    value_blocks = value_up.reshape(block_count, per_block, latent_share, value_width)
    column_start = lax.axis_index("ctx") * column_share

    def attend_block(blocks):
        latent_block, rotary_block, value_block = blocks
        gathered_latent, gathered_rotary = (
            lax.all_gather(latent_block, "ctx", axis=0, tiled=True),
            lax.all_gather(rotary_block, "ctx", axis=0, tiled=True),
        )
        scores = (
            jnp.einsum(
                "qhc,kc->qhk", gathered_latent, cache_latent, preferred_element_type=jnp.float32
            )
            + jnp.einsum(
                "qhr,kr->qhk", gathered_rotary, cache_rope, preferred_element_type=jnp.float32
            )
        ) * score_scale
        peaks = jnp.max(scores, axis=2)
        raised = jnp.exp(scores - peaks[:, :, None])
        totals = jnp.sum(raised, axis=2)
        weights = raised.astype(jnp.bfloat16)
        latent_out = jnp.einsum(
            "qhk,kc->qhc", weights, cache_latent, preferred_element_type=jnp.float32
        )
        projected = jnp.einsum(
            "qhc,hcv->qhv",
            latent_out,
            lax.all_gather(value_block, "ctx", axis=1, tiled=True).astype(jnp.float32),
            precision=lax.Precision.HIGHEST,
        )
        peak_all = lax.pmax(peaks, "ctx")
        factor = jnp.exp(peaks - peak_all)
        total_all = lax.psum(totals * factor, "ctx")
        scaled = projected * (factor / total_all)[:, :, None]
        head_full = lax.psum(scaled, "ctx").astype(jnp.bfloat16)
        return lax.dynamic_slice_in_dim(head_full, column_start, column_share, 2)

    column_blocks = lax.map(attend_block, (latent_blocks, rotary_blocks, value_blocks))
    every_row = column_blocks.shape[1]
    head_cols = jnp.transpose(column_blocks, (1, 0, 2, 3)).reshape(
        every_row, heads_here, column_share
    )
    own_rows = lax.psum_scatter(
        jnp.einsum("qhv,vhd->qd", head_cols, out_proj, preferred_element_type=jnp.float32),
        "ctx",
        scatter_dimension=0,
        tiled=True,
    )
    return lax.psum_scatter(own_rows, "head", scatter_dimension=1, tiled=True).astype(jnp.bfloat16)


def solution(mesh):
    return jax.shard_map(
        per_device,
        mesh=mesh,
        in_specs=(
            P(("groups", "ctx"), "head", None),
            P(("groups", "ctx"), "head", None),
            P(("groups", "ctx"), None),
            P(("groups", "ctx"), None),
            P("head", "ctx", None),
            P("ctx", "head", None),
        ),
        out_specs=P(("groups", "ctx"), "head"),
        check_vma=False,
    )
```

profile of v0, /device:TPU:0, one launch (start us, length us, event | category | flops | bytes accessed | tf_op | source)
XLA Modules:
  0.0 648.5 jit_solution(8575154838284618160)
XLA Ops:
  7.4 541.2 %while.12 = (s32[]{:T(128)}, bf16[4,8,8,16]{3,1,2,0:T(8,128)(2,1)S(1)}, bf16[4,8,64,128]{3,2,1,0:T(8,128)(2,1)}, bf16[4,1,8,512]{3,2,1,0:T(8,128)(2,1)}, bf16[25...) while((s32[]{:T(128)}, ...), condition=%wide.region_6.7_spmd, body=%wide.region_0.6_spmd.sunk | while | flops 86098176 | bytes 6291105 | solution.py:61
  7.4 1.6 constant_dynamic-slice_fusion.9
  9.0 0.7 constant_dynamic-slice_fusion.8
  9.6 27.8 %all-gather.7 = bf16[8,1,8,64]{3,2,1,0:T(8,128)(2,1)S(1)} all-gather(bf16[1,1,8,64]{3,2,1,0:T(8,128)(2,1)S(1)} %constant_dynamic-slice_fusion.8), channel_id=4, replica_groups=mesh['groups'=2,'ctx'=8,'head'=2] {'ctx'}, dimensions={0}, use_global_device_ids=true | all-gather | bytes 9216 | tf_op jit(solution)/shard_map/while/body/eval_jaxpr/all_gather | solution.py:31
  37.4 0.7 constant_dynamic-slice_fusion.7
  38.1 30.6 %all-gather.6 = bf16[8,1,8,512]{3,2,1,0:T(8,128)(2,1)S(1)} all-gather(bf16[1,1,8,512]{3,2,1,0:T(8,128)(2,1)S(1)} %constant_dynamic-slice_fusion.7), channel_id=3, replica_groups=mesh['groups'=2,'ctx'=8,'head'=2] {'ctx'}, dimensions={0}, use_global_device_ids=true | all-gather | bytes 73728 | tf_op jit(solution)/shard_map/while/body/eval_jaxpr/all_gather | solution.py:30
  68.7 1.2 fusion.41
  69.9 1.0 fusion.42
  70.8 19.8 %pmax.10 = f32[8,8]{1,0:T(8,128)S(1)} all-reduce(f32[8,8]{1,0:T(8,128)S(1)} %get-tuple-element.176), channel_id=1, replica_groups=mesh['groups'=2,'ctx'=8,'head'=2] {'ctx'}, use_global_device_ids=true, to_apply=%region_2.2 | all-reduce | flops 64 | bytes 512 | tf_op jit(solution)/shard_map/while/body/eval_jaxpr/pmax | solution.py:54
  90.6 0.2 fusion.43
  90.8 17.1 %psum.20 = f32[8,8]{1,0:T(8,128)S(1)} all-reduce(f32[8,8]{1,0:T(8,128)S(1)} %fusion.45), channel_id=1, replica_groups=mesh['groups'=2,'ctx'=8,'head'=2] {'ctx'}, use_global_device_ids=true, to_apply=%region_4.4 | all-reduce | flops 64 | bytes 512 | tf_op jit(solution)/shard_map/while/body/eval_jaxpr/psum | solution.py:56
  108.0 1.1 fusion.44
  109.2 1.7 fusion.47
  110.9 34.9 %psum.21 = bf16[8,8,128]{2,0,1:T(8,128)(2,1)S(1)} all-reduce(f32[8,8,128]{2,0,1:T(8,128)S(1)} %fusion.47), channel_id=1, replica_groups=mesh['groups'=2,'ctx'=8,'head'=2] {'ctx'}, use_global_device_ids=true, to_apply=%region_5.5 | all-reduce | flops 8192 | bytes 49152 | tf_op jit(solution)/shard_map/while/body/eval_jaxpr/psum | solution.py:58
  145.8 0.1 fusion.48
  145.9 1.6 constant_dynamic-slice_fusion.9
  147.5 0.7 constant_dynamic-slice_fusion.8
  148.2 26.1 %all-gather.7 = bf16[8,1,8,64]{3,2,1,0:T(8,128)(2,1)S(1)} all-gather(bf16[1,1,8,64]{3,2,1,0:T(8,128)(2,1)S(1)} %constant_dynamic-slice_fusion.8), channel_id=4, replica_groups=mesh['groups'=2,'ctx'=8,'head'=2] {'ctx'}, dimensions={0}, use_global_device_ids=true | all-gather | bytes 9216 | tf_op jit(solution)/shard_map/while/body/eval_jaxpr/all_gather | solution.py:31
  174.3 0.7 constant_dynamic-slice_fusion.7
  175.0 30.5 %all-gather.6 = bf16[8,1,8,512]{3,2,1,0:T(8,128)(2,1)S(1)} all-gather(bf16[1,1,8,512]{3,2,1,0:T(8,128)(2,1)S(1)} %constant_dynamic-slice_fusion.7), channel_id=3, replica_groups=mesh['groups'=2,'ctx'=8,'head'=2] {'ctx'}, dimensions={0}, use_global_device_ids=true | all-gather | bytes 73728 | tf_op jit(solution)/shard_map/while/body/eval_jaxpr/all_gather | solution.py:30
  205.5 1.2 fusion.41
  206.7 1.0 fusion.42
  207.6 17.2 %pmax.10 = f32[8,8]{1,0:T(8,128)S(1)} all-reduce(f32[8,8]{1,0:T(8,128)S(1)} %get-tuple-element.176), channel_id=1, replica_groups=mesh['groups'=2,'ctx'=8,'head'=2] {'ctx'}, use_global_device_ids=true, to_apply=%region_2.2 | all-reduce | flops 64 | bytes 512 | tf_op jit(solution)/shard_map/while/body/eval_jaxpr/pmax | solution.py:54
  224.8 0.2 fusion.43
  225.0 19.1 %psum.20 = f32[8,8]{1,0:T(8,128)S(1)} all-reduce(f32[8,8]{1,0:T(8,128)S(1)} %fusion.45), channel_id=1, replica_groups=mesh['groups'=2,'ctx'=8,'head'=2] {'ctx'}, use_global_device_ids=true, to_apply=%region_4.4 | all-reduce | flops 64 | bytes 512 | tf_op jit(solution)/shard_map/while/body/eval_jaxpr/psum | solution.py:56
  244.2 1.1 fusion.44
  245.3 1.7 fusion.47
  247.1 33.0 %psum.21 = bf16[8,8,128]{2,0,1:T(8,128)(2,1)S(1)} all-reduce(f32[8,8,128]{2,0,1:T(8,128)S(1)} %fusion.47), channel_id=1, replica_groups=mesh['groups'=2,'ctx'=8,'head'=2] {'ctx'}, use_global_device_ids=true, to_apply=%region_5.5 | all-reduce | flops 8192 | bytes 49152 | tf_op jit(solution)/shard_map/while/body/eval_jaxpr/psum | solution.py:58
  280.1 0.1 fusion.48
  280.2 1.6 constant_dynamic-slice_fusion.9
  281.8 0.7 constant_dynamic-slice_fusion.8
  282.5 26.1 %all-gather.7 = bf16[8,1,8,64]{3,2,1,0:T(8,128)(2,1)S(1)} all-gather(bf16[1,1,8,64]{3,2,1,0:T(8,128)(2,1)S(1)} %constant_dynamic-slice_fusion.8), channel_id=4, replica_groups=mesh['groups'=2,'ctx'=8,'head'=2] {'ctx'}, dimensions={0}, use_global_device_ids=true | all-gather | bytes 9216 | tf_op jit(solution)/shard_map/while/body/eval_jaxpr/all_gather | solution.py:31
  308.6 0.7 constant_dynamic-slice_fusion.7
  309.3 30.5 %all-gather.6 = bf16[8,1,8,512]{3,2,1,0:T(8,128)(2,1)S(1)} all-gather(bf16[1,1,8,512]{3,2,1,0:T(8,128)(2,1)S(1)} %constant_dynamic-slice_fusion.7), channel_id=3, replica_groups=mesh['groups'=2,'ctx'=8,'head'=2] {'ctx'}, dimensions={0}, use_global_device_ids=true | all-gather | bytes 73728 | tf_op jit(solution)/shard_map/while/body/eval_jaxpr/all_gather | solution.py:30
  339.8 1.2 fusion.41
  340.9 1.0 fusion.42
  341.9 17.2 %pmax.10 = f32[8,8]{1,0:T(8,128)S(1)} all-reduce(f32[8,8]{1,0:T(8,128)S(1)} %get-tuple-element.176), channel_id=1, replica_groups=mesh['groups'=2,'ctx'=8,'head'=2] {'ctx'}, use_global_device_ids=true, to_apply=%region_2.2 | all-reduce | flops 64 | bytes 512 | tf_op jit(solution)/shard_map/while/body/eval_jaxpr/pmax | solution.py:54
  359.1 0.2 fusion.43
  359.3 19.0 %psum.20 = f32[8,8]{1,0:T(8,128)S(1)} all-reduce(f32[8,8]{1,0:T(8,128)S(1)} %fusion.45), channel_id=1, replica_groups=mesh['groups'=2,'ctx'=8,'head'=2] {'ctx'}, use_global_device_ids=true, to_apply=%region_4.4 | all-reduce | flops 64 | bytes 512 | tf_op jit(solution)/shard_map/while/body/eval_jaxpr/psum | solution.py:56
  378.4 1.1 fusion.44
  379.6 1.7 fusion.47
  381.3 33.0 %psum.21 = bf16[8,8,128]{2,0,1:T(8,128)(2,1)S(1)} all-reduce(f32[8,8,128]{2,0,1:T(8,128)S(1)} %fusion.47), channel_id=1, replica_groups=mesh['groups'=2,'ctx'=8,'head'=2] {'ctx'}, use_global_device_ids=true, to_apply=%region_5.5 | all-reduce | flops 8192 | bytes 49152 | tf_op jit(solution)/shard_map/while/body/eval_jaxpr/psum | solution.py:58
  414.3 0.1 fusion.48
  414.5 1.6 constant_dynamic-slice_fusion.9
  416.0 0.7 constant_dynamic-slice_fusion.8
  416.7 26.0 %all-gather.7 = bf16[8,1,8,64]{3,2,1,0:T(8,128)(2,1)S(1)} all-gather(bf16[1,1,8,64]{3,2,1,0:T(8,128)(2,1)S(1)} %constant_dynamic-slice_fusion.8), channel_id=4, replica_groups=mesh['groups'=2,'ctx'=8,'head'=2] {'ctx'}, dimensions={0}, use_global_device_ids=true | all-gather | bytes 9216 | tf_op jit(solution)/shard_map/while/body/eval_jaxpr/all_gather | solution.py:31
  442.7 0.7 constant_dynamic-slice_fusion.7
  443.4 30.5 %all-gather.6 = bf16[8,1,8,512]{3,2,1,0:T(8,128)(2,1)S(1)} all-gather(bf16[1,1,8,512]{3,2,1,0:T(8,128)(2,1)S(1)} %constant_dynamic-slice_fusion.7), channel_id=3, replica_groups=mesh['groups'=2,'ctx'=8,'head'=2] {'ctx'}, dimensions={0}, use_global_device_ids=true | all-gather | bytes 73728 | tf_op jit(solution)/shard_map/while/body/eval_jaxpr/all_gather | solution.py:30
  473.9 1.2 fusion.41
  475.1 1.0 fusion.42
  476.0 17.2 %pmax.10 = f32[8,8]{1,0:T(8,128)S(1)} all-reduce(f32[8,8]{1,0:T(8,128)S(1)} %get-tuple-element.176), channel_id=1, replica_groups=mesh['groups'=2,'ctx'=8,'head'=2] {'ctx'}, use_global_device_ids=true, to_apply=%region_2.2 | all-reduce | flops 64 | bytes 512 | tf_op jit(solution)/shard_map/while/body/eval_jaxpr/pmax | solution.py:54
  493.2 0.2 fusion.43
  493.4 19.1 %psum.20 = f32[8,8]{1,0:T(8,128)S(1)} all-reduce(f32[8,8]{1,0:T(8,128)S(1)} %fusion.45), channel_id=1, replica_groups=mesh['groups'=2,'ctx'=8,'head'=2] {'ctx'}, use_global_device_ids=true, to_apply=%region_4.4 | all-reduce | flops 64 | bytes 512 | tf_op jit(solution)/shard_map/while/body/eval_jaxpr/psum | solution.py:56
  512.6 1.1 fusion.44
  513.7 1.7 fusion.47
  515.5 33.0 %psum.21 = bf16[8,8,128]{2,0,1:T(8,128)(2,1)S(1)} all-reduce(f32[8,8,128]{2,0,1:T(8,128)S(1)} %fusion.47), channel_id=1, replica_groups=mesh['groups'=2,'ctx'=8,'head'=2] {'ctx'}, use_global_device_ids=true, to_apply=%region_5.5 | all-reduce | flops 8192 | bytes 49152 | tf_op jit(solution)/shard_map/while/body/eval_jaxpr/psum | solution.py:58
  548.5 0.1 fusion.48
  548.6 7.7 %convolution_bitcast_fusion.1 = f32[8,7168]{1,0:T(8,128)} fusion(bf16[8,32,16]{2,0,1:T(8,128)(2,1)S(1)} %bitcast.65, bf16[16,32,7168]{2,1,0:T(8,128)(2,1)} %param.13), kind=kOutput, calls=%fused_computation.25 | convolution fusion | flops 58720256 | bytes 7577600 | tf_op jit(solution)/shard_map/qhv,vhd->qd/dot_general | solution.py:67
  556.4 0.6 dynamic-slice
  557.0 66.9 %all-reduce.3.cloned.1.call-done = f32[8,7168]{1,0:T(8,128)} async-done(((f32[8,7168]{1,0:T(8,128)}), f32[8,7168]{1,0:T(8,128)}) %all-reduce.3.cloned.1.call-update) | async-done | bytes 229392
  623.9 1.6 constant_dynamic-slice_fusion.3
  625.5 2.4 copy.14
  628.0 10.8 %reduce-scatter.4.cloned.1.call-done = f32[3584,1]{1,0:T(8,128)} async-done(((f32[7168,1]{1,0:T(8,128)}), f32[3584,1]{1,0:T(8,128)}) %reduce-scatter.4.cloned.1.call-update) | async-done | bytes 14352
  638.8 2.7 copy.15
  (31 shorter events, 0.7 us)
Async XLA Ops:
  7.4 101.8 %all-gather.11.cloned.1.call-start = ((), (), s32[]{:S(2)}) async-start(), calls=%async_computation.3 | async-start | bytes 1179648 | tf_op jit(solution)/shard_map/while/body/eval_jaxpr/all_gather | solution.py:51
  145.9 99.4 %all-gather.11.cloned.1.call-start = ((), (), s32[]{:S(2)}) async-start(), calls=%async_computation.3 | async-start | bytes 1179648 | tf_op jit(solution)/shard_map/while/body/eval_jaxpr/all_gather | solution.py:51
  280.2 99.4 %all-gather.11.cloned.1.call-start = ((), (), s32[]{:S(2)}) async-start(), calls=%async_computation.3 | async-start | bytes 1179648 | tf_op jit(solution)/shard_map/while/body/eval_jaxpr/all_gather | solution.py:51
  414.4 99.3 %all-gather.11.cloned.1.call-start = ((), (), s32[]{:S(2)}) async-start(), calls=%async_computation.3 | async-start | bytes 1179648 | tf_op jit(solution)/shard_map/while/body/eval_jaxpr/all_gather | solution.py:51
  548.6 7.8 %copy-start = (u32[32]{0:T(128)S(1)}, u32[32]{0:T(128)}, u32[]{:S(2)}) copy-start(u32[32]{0:T(128)} %constant.54) | copy-start | bytes 388
  548.6 75.3 %all-reduce.3.cloned.1.call-start = ((), (), s32[]{:S(2)}) async-start(), calls=%async_computation.2 | async-start | bytes 458752
  556.4 82.4 %reduce-scatter.4.cloned.1.call-start = ((), (), s32[]{:S(2)}) async-start(), calls=%async_computation.1 | async-start | bytes 5505024
Sparse Core Ops, SparseCore 0:
  10.4 43.0 all-gather.10
  148.9 37.5 all-gather.10
  283.2 37.4 all-gather.10
  417.1 37.3 all-gather.10
Sparse Core Ops, SparseCore 1:
  556.5 67.4 all-reduce.2
  628.1 10.6 reduce-scatter.3
where the time goes:
time: 650 us; the launch traced here: 649 us
  blocking collectives  508 us (78%)
  waiting for transfers between devices  77.8 us (12%)
  matrix products  27.6 us (4%)
  local copies, waits for them, and re-layouts  19.7 us (3%)
  between operations  14.5 us (2%)
    psum x4, blocking collectives, attend_block(): head_full = lax.psum(scaled, 'ctx').astype(jnp.bfloat16)  134 us
    all_gather x4, blocking collectives, attend_block(): lax.all_gather(latent_block, 'ctx', axis=0, tiled=True)  122 us
    all_gather x4, blocking collectives, attend_block(): lax.all_gather(rotary_block, 'ctx', axis=0, tiled=True)  106 us
    unnamed x4, waiting for transfers between devices  77.7 us
    psum x4, blocking collectives, attend_block(): total_all = lax.psum(totals * factor, 'ctx')  74.4 us
    pmax x4, blocking collectives, attend_block(): peak_all = lax.pmax(peaks, 'ctx')  71.4 us
  transfers between devices with their start and end apart: 6, of which 2 were waited for; matrix products, arithmetic and copies ran while one was open for 3% of the time, Pallas kernels for 0%

commit v1 on v0

--- a/solution.py
+++ b/solution.py
@@ -1,13 +1,270 @@
+import functools
+
 import jax
 import jax.numpy as jnp
 from jax import lax
+from jax.experimental import pallas as pl
+from jax.experimental.pallas import tpu as pltpu
 from jax.sharding import PartitionSpec as P
 
 ROPE = 64
 NOPE = 128
+SCALE = (NOPE + ROPE) ** (-0.5)
+F32 = jnp.float32
+BF16 = jnp.bfloat16
+MESH = pl.DeviceIdType.MESH
+STAT = 16
+
+
+def contract(a, b, da, db):
+    return lax.dot_general(a, b, (((da,), (db,)), ((), ())), preferred_element_type=F32)
+
+
+def kernel(
+    n, ql, qr, cl, cr, vu, wo, out,
+    qlb, qrb, clb, crb, vub, wob,
+    lat_send, lat_recv, comb, proj, pr_send, pr_recv, att, at_send, at_recv,
+    local_sem, q_send, q_recv, c_send, c_recv, l_send, l_recv, p_send, p_recv, a_send, a_recv,
+):
+    me = lax.axis_index("ctx")
+    hd = lax.axis_index("head")
+    half = n // 2
+    z = me // 2
+    x = me % 2
+    partner = 2 * z + 1 - x
+    heads = ql.shape[1]
+    tokens = cl.shape[0]
+    share = vu.shape[1]
+    cols = lat_send.shape[2]
+    vshare = pr_send.shape[1]
+    rows = proj.shape[0]
+    chunks = out.shape[1] // 128
+    pad = at_send.shape[2]
+
+    own = pl.ds(0, tokens)
+    local = [
+        pltpu.make_async_copy(cl, clb.at[own], local_sem.at[0]),
+        pltpu.make_async_copy(cr, crb.at[own], local_sem.at[1]),
+        pltpu.make_async_copy(ql.at[0], qlb.at[z], local_sem.at[2]),
+        pltpu.make_async_copy(qr.at[0], qrb.at[z], local_sem.at[3]),
+        pltpu.make_async_copy(vu, vub, local_sem.at[4]),
+        pltpu.make_async_copy(wo, wob, local_sem.at[5]),
+    ]
+    for copy in local:
+        copy.start()
+
+    barrier = pltpu.get_barrier_semaphore()
+    for e in range(2):
+        for d in range(n):
+            if e or d:
+                pl.semaphore_signal(
+                    barrier, inc=1, device_id={"ctx": (me + d) % n, "head": (hd + e) % 2},
+                    device_id_type=MESH,
+                )
+    pl.semaphore_wait(barrier, 2 * n - 1)
+
+    part = tokens // 2
+    mine = pl.ds(pl.multiple_of(hd * part, part), part)
+    there = pl.ds(pl.multiple_of(tokens + hd * part, part), part)
+    cache = [
+        pltpu.make_async_remote_copy(
+            src.at[mine], dst.at[there], c_send.at[k], c_recv.at[k],
+            device_id={"ctx": partner}, device_id_type=MESH,
+        )
+        for k, (src, dst) in enumerate(((cl, clb), (cr, crb)))
+    ]
+    queries = []
+    for d in range(1, half):
+        peer = 2 * ((z + d) % half) + x
+        for k, (src, dst) in enumerate(((ql, qlb), (qr, qrb))):
+            queries.append(
+                pltpu.make_async_remote_copy(
+                    src.at[0], dst.at[z], q_send.at[k, d], q_recv.at[k, d],
+                    device_id={"ctx": peer}, device_id_type=MESH,
+                )
+            )
+    for copy in cache + queries:
+        copy.start()
+
+    for copy in local[:4]:
+        copy.wait()
+    for copy in cache:
+        copy.wait_recv()
+    swap = [
+        pltpu.make_async_remote_copy(
+            dst.at[there], dst.at[there], c_send.at[2 + k], c_recv.at[2 + k],
+            device_id={"head": 1 - hd}, device_id_type=MESH,
+        )
+        for k, dst in enumerate((clb, crb))
+    ]
+    for copy in swap:
+        copy.start()
+    for copy in queries:
+        copy.wait_recv()
+
+    q = qlb[...].reshape(cols, qlb.shape[2])
+    r = qrb[...].reshape(cols, qrb.shape[2])
+    first = contract(clb[0:tokens], q, 1, 1) + contract(crb[0:tokens], r, 1, 1)
+    for copy in swap:
+        copy.wait_recv()
+    second = contract(clb[tokens : 2 * tokens], q, 1, 1) + contract(crb[tokens : 2 * tokens], r, 1, 1)
+    scores = jnp.concatenate([first, second], axis=0) * SCALE
+    peak = jnp.max(scores, axis=0, keepdims=True).astype(BF16).astype(F32)
+    raised = jnp.exp(scores - peak)
+    total = jnp.sum(raised, axis=0, keepdims=True)
+    latent = contract(clb[...], raised.astype(BF16), 0, 0)
+    high = total.astype(BF16).astype(F32)
+    row = lax.broadcasted_iota(jnp.int32, (STAT, cols), 0)
+    stats = jnp.where(
+        row == 0, peak, jnp.where(row == 1, high, jnp.where(row == 2, total - high, 0.0))
+    ).astype(BF16)
+    for j in range(n):
+        lat_send[j, 0:share, :] = latent[j * share : (j + 1) * share].astype(BF16)
+        lat_send[j, share : share + STAT, :] = stats
+
+    def exchange(send, recv, send_sem, recv_sem):
+        copies = []
+        for d in range(1, n):
+            peer = (me + d) % n
+            copy = pltpu.make_async_remote_copy(
+                send.at[peer], recv.at[me], send_sem.at[d], recv_sem.at[d],
+                device_id={"ctx": peer}, device_id_type=MESH,
+            )
+            copy.start()
+            copies.append(copy)
+        recv[me] = send[me]
+        for copy in copies:
+            copy.wait_recv()
+        return copies
+
+    lat_copies = exchange(lat_send, lat_recv, l_send, l_recv)
+
+    sides = []
+    for side in range(2):
+        blocks = [lat_recv[2 * k + side].astype(F32) for k in range(half)]
+        peaks = [b[share : share + 1] for b in blocks]
+        top = functools.reduce(jnp.maximum, peaks)
+        factors = [jnp.exp(p - top) for p in peaks]
+        whole = sum(f * (b[share + 1 : share + 2] + b[share + 2 : share + 3]) for f, b in zip(factors, blocks))
+        sides.append(sum(f * b[0:share] for f, b in zip(factors, blocks)) / whole)
+    comb[...] = jnp.concatenate(sides, axis=1).T
+
+    local[4].wait()
+    for h in range(heads):
+        lhs = comb[pl.ds(h, n, stride=heads), :].astype(BF16)
+        proj[pl.ds(h, n, stride=heads), :] = jnp.dot(lhs, vub[h], preferred_element_type=F32)
+    flipped = proj[...].T
+    for j in range(n):
+        pr_send[j] = flipped[j * vshare : (j + 1) * vshare].astype(BF16)
+    pr_copies = exchange(pr_send, pr_recv, p_send, p_recv)
+
+    head_out = sum(pr_recv[s].astype(F32) for s in range(n)).astype(BF16)
+    wide = vshare * heads
+    spread = (
+        lax.broadcasted_iota(jnp.int32, (vshare, wide), 1) // heads
+        == lax.broadcasted_iota(jnp.int32, (vshare, wide), 0)
+    ).astype(F32).astype(BF16)
+    copied = contract(head_out, spread, 0, 0)
+    keep = (
+        lax.broadcasted_iota(jnp.int32, (rows, wide), 1) % heads
+        == lax.broadcasted_iota(jnp.int32, (rows, wide), 0) % heads
+    )
+    lhs = jnp.sum(jnp.where(keep, copied, 0.0).reshape(n, heads, wide), axis=1).astype(BF16)
+
+    local[5].wait()
+    for k in range(2):
+        for c in range(chunks):
+            at = (k * chunks + c) * 128
+            att[pl.ds(k * n * pad + c, n, stride=pad), :] = jnp.dot(
+                lhs, wob[:, at : at + 128], preferred_element_type=F32
+            )
+        for c in range(chunks, pad):
+            att[pl.ds(k * n * pad + c, n, stride=pad), :] = jnp.zeros((n, 128), F32)
+    for k in range(2):
+        for j in range(n):
+            slot = (j % 2) * half + j // 2
+            at = (k * n + slot) * pad
+            at_send[k, j] = att[at : at + pad, :].astype(BF16)
+
+    at_copies = []
+    for e in (1, 0):
+        for d in range(n):
+            if e or d:
+                peer = (me + d) % n
+                other = (hd + e) % 2
+                copy = pltpu.make_async_remote_copy(
+                    at_send.at[other, peer], at_recv.at[hd, me], a_send.at[e, d], a_recv.at[e, d],
+                    device_id={"ctx": peer, "head": other}, device_id_type=MESH,
+                )
+                copy.start()
+                at_copies.append(copy)
+    at_recv[hd, me] = at_send[hd, me]
+    for copy in at_copies:
+        copy.wait_recv()
+    result = sum(at_recv[k, s].astype(F32) for k in range(2) for s in range(n)).astype(BF16)
+    for c in range(chunks):
+        out[0:1, c * 128 : (c + 1) * 128] = result[c : c + 1, :]
+
+    for copy in cache + queries + swap + lat_copies + pr_copies + at_copies:
+        copy.wait_send()
+
+
+def fused(n, query_latent, query_rope, cache_latent, cache_rope, value_up, out_proj):
+    heads, latent_width = query_latent.shape[1:]
+    rotary = query_rope.shape[2]
+    tokens = cache_latent.shape[0]
+    share, value_width = value_up.shape[1:]
+    vshare, _, width = out_proj.shape
+    half = n // 2
+    cols = half * heads
+    rows = n * heads
+    mine = width // 2
+    pad = -(-(mine // 128) // 16) * 16
+    wide = vshare * heads
+    dma = pltpu.SemaphoreType.DMA
+    any_spec = pl.BlockSpec(memory_space=pl.ANY)
+    return pl.pallas_call(
+        functools.partial(kernel, n),
+        out_shape=jax.ShapeDtypeStruct((1, mine), BF16),
+        in_specs=[any_spec] * 6,
+        out_specs=pl.BlockSpec(memory_space=pltpu.VMEM),
+        scratch_shapes=[
+            pltpu.VMEM((half, heads, latent_width), BF16),
+            pltpu.VMEM((half, heads, rotary), BF16),
+            pltpu.VMEM((2 * tokens, latent_width), BF16),
+            pltpu.VMEM((2 * tokens, rotary), BF16),
+            pltpu.VMEM(value_up.shape, BF16),
+            pltpu.VMEM((wide, width), BF16),
+            pltpu.VMEM((n, share + STAT, cols), BF16),
+            pltpu.VMEM((n, share + STAT, cols), BF16),
+            pltpu.VMEM((rows, share), F32),
+            pltpu.VMEM((rows, value_width), F32),
+            pltpu.VMEM((n, vshare, rows), BF16),
+            pltpu.VMEM((n, vshare, rows), BF16),
+            pltpu.VMEM((2 * n * pad, 128), F32),
+            pltpu.VMEM((2, n, pad, 128), BF16),
+            pltpu.VMEM((2, n, pad, 128), BF16),
+            dma((6,)),
+            dma((2, half)), dma((2, half)),
+            dma((4,)), dma((4,)),
+            dma((n,)), dma((n,)),
+            dma((n,)), dma((n,)),
+            dma((2, n)), dma((2, n)),
+        ],
+        compiler_params=pltpu.CompilerParams(
+            collective_id=0, has_side_effects=True, vmem_limit_bytes=56 * 2**20
+        ),
+    )(query_latent, query_rope, cache_latent, cache_rope, value_up, out_proj.reshape(wide, width))
 
 
 def per_device(query_latent, query_rope, cache_latent, cache_rope, value_up, out_proj):
+    n = lax.axis_size("ctx")
+    if n % 2 == 0 and n <= 16 and value_up.shape[1] % 16 == 0 and out_proj.shape[0] % 16 == 0:
+        return fused(n, query_latent, query_rope, cache_latent, cache_rope, value_up, out_proj)
+    return plain(query_latent, query_rope, cache_latent, cache_rope, value_up, out_proj)
+
+
+def plain(query_latent, query_rope, cache_latent, cache_rope, value_up, out_proj):
     score_scale = (NOPE + ROPE) ** (-0.5)
     rows_here, heads_here, latent_width = query_latent.shape
     rotary_width = query_rope.shape[2]

time: 650 us -> 33.9 us (0.05)
  blocking collectives: 508 us -> 0 us
  waiting for transfers between devices: 77.8 us -> 0 us
  Pallas kernels: 0 us -> 30.9 us
  matrix products: 27.6 us -> 0 us
  local copies, waits for them, and re-layouts: 19.7 us -> 2.81 us
  between operations: 14.5 us -> 0.01 us
    all_gather x8 -> x0, blocking collectives: 228 us -> none  [the longest x4 122 us: attend_block(): lax.all_gather(latent_block, 'ctx', axis=0, tiled=True)]
    psum x8 -> x0, blocking collectives: 208 us -> none  [the longest x4 134 us: attend_block(): head_full = lax.psum(scaled, 'ctx').astype(jnp.bfloat16)]
    unnamed x4 -> x0, waiting for transfers between devices: 77.7 us -> none
    pmax x4 -> x0, blocking collectives: 71.4 us -> none  [attend_block(): peak_all = lax.pmax(peaks, 'ctx')]
    pallas_call x0 -> x1, Pallas kernels: none -> 30.9 us  [fused(): pl.pallas_call(functools.partial(kernel, n), out_shape=jax.ShapeDtypeStru...]
    dot_general x17 -> x0, matrix products: 27.6 us -> none  [the longest x1 7.7 us: per_device(): jnp.einsum('qhv,vhd->qd', head_cols, out_proj, preferred_element_type=jnp...]
    dynamic_slice x12 -> x0, local copies, waits for them, and re-layouts: 11.8 us -> none  [per_device(): lax.map(attend_block, (latent_blocks, rotary_blocks, value_blocks))]
  transfers between devices with their start and end apart: 6 -> 0, of which waited for: 2 -> 0; matrix products, arithmetic and copies ran while one was open for 3% -> 0% of each run, Pallas kernels for 0% -> 0%
where the time goes in v1:
time: 33.9 us; the launch traced here: 33.7 us
  Pallas kernels  30.9 us (91%)
  local copies, waits for them, and re-layouts  2.81 us (8%)
    pallas_call x1, Pallas kernels, fused(): pl.pallas_call(functools.partial(kernel, n), out_shape=jax.ShapeDtypeStru...  30.9 us
    unnamed x2, local copies, waits for them, and re-layouts  2.81 us

profile of v1, /device:TPU:0, one launch (start us, length us, event | category | flops | bytes accessed | tf_op | source)
XLA Modules:
  0.0 33.7 jit_solution(1562366998524884258)
XLA Ops:
  0.0 1.5 %copy.7.cr = bf16[256,64]{1,0:T(8,128)(2,1)} copy(bf16[256,64]{0,1:T(8,128)(2,1)} %param.9) | data formatting | bytes 65536 | tf_op args[3]
  1.5 30.9 %shard_map.64 = bf16[1,3584]{1,0:T(2,128)(2,1)} custom-call(bf16[1,32,512]{2,1,0:T(8,128)(2,1)} %ql.1, bf16[1,32,64]{2,1,0:T(8,128)(2,1)} %qr.1, bf16[256,512]{1,0:T(8,128)(2,1)} %cl.1, bf16[256,64]{1,0:T(8,128)(2,1)} %copy.7.cr, bf16[32,64,128]{2,1,0:T(8,128)(2,1)} %vu.1, bf16[512,7168]{1,0:T(8,128)(2,1)} %bitcast.1), custom_call_target="tpu_custom_call" | custom-call | tf_op jit(solution)/shard_map/pallas_call | solution.py:226
  32.4 1.3 %copy.9 = bf16[1,3584]{1,0:T(2,128)(2,1)} copy(bf16[1,3584]{1,0:T(2,128)(2,1)} %shard_map.64) | data formatting | bytes 14336

commit v2 on v1

--- a/solution.py
+++ b/solution.py
@@ -13,6 +13,7 @@
 F32 = jnp.float32
 BF16 = jnp.bfloat16
 MESH = pl.DeviceIdType.MESH
+PIECES = 4
 STAT = 16
 
 
@@ -20,11 +21,15 @@
     return lax.dot_general(a, b, (((da,), (db,)), ((), ())), preferred_element_type=F32)
 
 
+def far_first(n):
+    return sorted(range(1, n), key=lambda d: abs(d - n // 2))
+
+
 def kernel(
     n, ql, qr, cl, cr, vu, wo, out,
-    qlb, qrb, clb, crb, vub, wob,
-    lat_send, lat_recv, comb, proj, pr_send, pr_recv, att, at_send, at_recv,
-    local_sem, q_send, q_recv, c_send, c_recv, l_send, l_recv, p_send, p_recv, a_send, a_recv,
+    qlb, qrb, clb, crb, clt, vub, vut, wob,
+    lat_send, lat_recv, pr_send, pr_recv, att, at_send, at_recv,
+    local_sem, q_send, q_recv, c_send, c_recv, s_send, s_recv, l_send, l_recv, p_send, p_recv, a_send, a_recv,
 ):
     me = lax.axis_index("ctx")
     hd = lax.axis_index("head")
@@ -37,14 +42,14 @@
     share = vu.shape[1]
     cols = lat_send.shape[2]
     vshare = pr_send.shape[1]
-    rows = proj.shape[0]
+    rows = pr_send.shape[2]
     chunks = out.shape[1] // 128
     pad = at_send.shape[2]
 
     own = pl.ds(0, tokens)
     local = [
         pltpu.make_async_copy(cl, clb.at[own], local_sem.at[0]),
-        pltpu.make_async_copy(cr, crb.at[own], local_sem.at[1]),
+        pltpu.make_async_copy(cr, crb.at[:, own], local_sem.at[1]),
         pltpu.make_async_copy(ql.at[0], qlb.at[z], local_sem.at[2]),
         pltpu.make_async_copy(qr.at[0], qrb.at[z], local_sem.at[3]),
         pltpu.make_async_copy(vu, vub, local_sem.at[4]),
@@ -54,28 +59,30 @@
         copy.start()
 
     barrier = pltpu.get_barrier_semaphore()
-    for e in range(2):
-        for d in range(n):
-            if e or d:
-                pl.semaphore_signal(
-                    barrier, inc=1, device_id={"ctx": (me + d) % n, "head": (hd + e) % 2},
-                    device_id_type=MESH,
-                )
-    pl.semaphore_wait(barrier, 2 * n - 1)
+    line = [2 * ((z + d) % half) + x for d in far_first(half)]
+    for peer in line:
+        pl.semaphore_signal(barrier, inc=1, device_id={"ctx": peer}, device_id_type=MESH)
+    pl.semaphore_signal(barrier, inc=1, device_id={"ctx": partner}, device_id_type=MESH)
+    pl.semaphore_signal(barrier, inc=1, device_id={"head": 1 - hd}, device_id_type=MESH)
+    pl.semaphore_wait(barrier, len(line) + 2)
 
     part = tokens // 2
-    mine = pl.ds(pl.multiple_of(hd * part, part), part)
-    there = pl.ds(pl.multiple_of(tokens + hd * part, part), part)
+    piece = part // PIECES
+    spans = [(cr.at[:, pl.ds(pl.multiple_of(hd * part, part), part)],
+              crb.at[:, pl.ds(pl.multiple_of(tokens + hd * part, part), part)])]
+    for k in range(PIECES):
+        spans.append((
+            cl.at[pl.ds(pl.multiple_of(hd * part + k * piece, piece), piece)],
+            clb.at[pl.ds(pl.multiple_of(tokens + hd * part + k * piece, piece), piece)],
+        ))
     cache = [
         pltpu.make_async_remote_copy(
-            src.at[mine], dst.at[there], c_send.at[k], c_recv.at[k],
-            device_id={"ctx": partner}, device_id_type=MESH,
-        )
-        for k, (src, dst) in enumerate(((cl, clb), (cr, crb)))
+            src, dst, c_send.at[k], c_recv.at[k], device_id={"ctx": partner}, device_id_type=MESH
+        )
+        for k, (src, dst) in enumerate(spans)
     ]
     queries = []
-    for d in range(1, half):
-        peer = 2 * ((z + d) % half) + x
+    for d, peer in enumerate(line):
         for k, (src, dst) in enumerate(((ql, qlb), (qr, qrb))):
             queries.append(
                 pltpu.make_async_remote_copy(
@@ -83,36 +90,39 @@
                     device_id={"ctx": peer}, device_id_type=MESH,
                 )
             )
-    for copy in cache + queries:
+    for copy in queries + cache:
         copy.start()
 
-    for copy in local[:4]:
+    for copy in local[:5]:
         copy.wait()
-    for copy in cache:
-        copy.wait_recv()
-    swap = [
-        pltpu.make_async_remote_copy(
-            dst.at[there], dst.at[there], c_send.at[2 + k], c_recv.at[2 + k],
-            device_id={"head": 1 - hd}, device_id_type=MESH,
-        )
-        for k, dst in enumerate((clb, crb))
-    ]
-    for copy in swap:
+    clt[...] = clb[0:tokens].T
+    vut[...] = vub[...].reshape(heads * share, vut.shape[0]).T
+
+    swap = []
+    for k, (_, dst) in enumerate(spans):
+        cache[k].wait_recv()
+        copy = pltpu.make_async_remote_copy(
+            dst, dst, s_send.at[k], s_recv.at[k], device_id={"head": 1 - hd}, device_id_type=MESH
+        )
         copy.start()
+        swap.append(copy)
     for copy in queries:
         copy.wait_recv()
 
     q = qlb[...].reshape(cols, qlb.shape[2])
     r = qrb[...].reshape(cols, qrb.shape[2])
-    first = contract(clb[0:tokens], q, 1, 1) + contract(crb[0:tokens], r, 1, 1)
+    first = contract(clb[0:tokens], q, 1, 1) + contract(crb[:, 0:tokens], r, 0, 1)
     for copy in swap:
         copy.wait_recv()
-    second = contract(clb[tokens : 2 * tokens], q, 1, 1) + contract(crb[tokens : 2 * tokens], r, 1, 1)
+    second = contract(clb[tokens : 2 * tokens], q, 1, 1) + contract(crb[:, tokens : 2 * tokens], r, 0, 1)
     scores = jnp.concatenate([first, second], axis=0) * SCALE
     peak = jnp.max(scores, axis=0, keepdims=True).astype(BF16).astype(F32)
     raised = jnp.exp(scores - peak)
     total = jnp.sum(raised, axis=0, keepdims=True)
-    latent = contract(clb[...], raised.astype(BF16), 0, 0)
+    weights = raised.astype(BF16)
+    latent = contract(clt[...], weights[0:tokens], 1, 0) + contract(
+        clb[tokens : 2 * tokens], weights[tokens : 2 * tokens], 0, 0
+    )
     high = total.astype(BF16).astype(F32)
     row = lax.broadcasted_iota(jnp.int32, (STAT, cols), 0)
     stats = jnp.where(
@@ -124,7 +134,7 @@
 
     def exchange(send, recv, send_sem, recv_sem):
         copies = []
-        for d in range(1, n):
+        for d in far_first(n):
             peer = (me + d) % n
             copy = pltpu.make_async_remote_copy(
                 send.at[peer], recv.at[me], send_sem.at[d], recv_sem.at[d],
@@ -147,13 +157,18 @@
         factors = [jnp.exp(p - top) for p in peaks]
         whole = sum(f * (b[share + 1 : share + 2] + b[share + 2 : share + 3]) for f, b in zip(factors, blocks))
         sides.append(sum(f * b[0:share] for f, b in zip(factors, blocks)) / whole)
-    comb[...] = jnp.concatenate(sides, axis=1).T
-
-    local[4].wait()
-    for h in range(heads):
-        lhs = comb[pl.ds(h, n, stride=heads), :].astype(BF16)
-        proj[pl.ds(h, n, stride=heads), :] = jnp.dot(lhs, vub[h], preferred_element_type=F32)
-    flipped = proj[...].T
+    comb = jnp.concatenate(sides, axis=1)
+
+    per = max(256 // share, 1)
+    stacked = jnp.concatenate([comb] * per, axis=0)
+    lane = lax.broadcasted_iota(jnp.int32, stacked.shape, 1) % heads
+    block = lax.broadcasted_iota(jnp.int32, stacked.shape, 0) // share
+    flipped = jnp.zeros((vut.shape[0], rows), F32)
+    for g in range(heads // per):
+        rhs = jnp.where(lane == block + g * per, stacked, 0.0).astype(BF16)
+        flipped += jnp.dot(
+            vut[:, g * per * share : (g + 1) * per * share], rhs, preferred_element_type=F32
+        )
     for j in range(n):
         pr_send[j] = flipped[j * vshare : (j + 1) * vshare].astype(BF16)
     pr_copies = exchange(pr_send, pr_recv, p_send, p_recv)
@@ -172,32 +187,28 @@
     lhs = jnp.sum(jnp.where(keep, copied, 0.0).reshape(n, heads, wide), axis=1).astype(BF16)
 
     local[5].wait()
-    for k in range(2):
-        for c in range(chunks):
-            at = (k * chunks + c) * 128
-            att[pl.ds(k * n * pad + c, n, stride=pad), :] = jnp.dot(
-                lhs, wob[:, at : at + 128], preferred_element_type=F32
-            )
+    step = 256 if chunks % 2 == 0 else 128
+    at_copies = []
+    for e in (1, 0):
+        other = (hd + e) % 2
+        for c in range(chunks * 128 // step):
+            at = pl.multiple_of(other * chunks * 128 + c * step, 128)
+            value = jnp.dot(lhs, wob[:, pl.ds(at, step)], preferred_element_type=F32)
+            for t in range(step // 128):
+                att[pl.ds(c * (step // 128) + t, n, stride=pad), :] = value[:, t * 128 : (t + 1) * 128]
         for c in range(chunks, pad):
-            att[pl.ds(k * n * pad + c, n, stride=pad), :] = jnp.zeros((n, 128), F32)
-    for k in range(2):
+            att[pl.ds(c, n, stride=pad), :] = jnp.zeros((n, 128), F32)
         for j in range(n):
             slot = (j % 2) * half + j // 2
-            at = (k * n + slot) * pad
-            at_send[k, j] = att[at : at + pad, :].astype(BF16)
-
-    at_copies = []
-    for e in (1, 0):
-        for d in range(n):
-            if e or d:
-                peer = (me + d) % n
-                other = (hd + e) % 2
-                copy = pltpu.make_async_remote_copy(
-                    at_send.at[other, peer], at_recv.at[hd, me], a_send.at[e, d], a_recv.at[e, d],
-                    device_id={"ctx": peer, "head": other}, device_id_type=MESH,
-                )
-                copy.start()
-                at_copies.append(copy)
+            at_send[other, j] = att[slot * pad : (slot + 1) * pad, :].astype(BF16)
+        for d in far_first(n) + [0] * e:
+            peer = (me + d) % n
+            copy = pltpu.make_async_remote_copy(
+                at_send.at[other, peer], at_recv.at[hd, me], a_send.at[e, d], a_recv.at[e, d],
+                device_id={"ctx": peer, "head": other}, device_id_type=MESH,
+            )
+            copy.start()
+            at_copies.append(copy)
     at_recv[hd, me] = at_send[hd, me]
     for copy in at_copies:
         copy.wait_recv()
@@ -232,21 +243,22 @@
             pltpu.VMEM((half, heads, latent_width), BF16),
             pltpu.VMEM((half, heads, rotary), BF16),
             pltpu.VMEM((2 * tokens, latent_width), BF16),
-            pltpu.VMEM((2 * tokens, rotary), BF16),
+            pltpu.VMEM((rotary, 2 * tokens), BF16),
+            pltpu.VMEM((latent_width, tokens), BF16),
             pltpu.VMEM(value_up.shape, BF16),
+            pltpu.VMEM((value_width, heads * share), BF16),
             pltpu.VMEM((wide, width), BF16),
             pltpu.VMEM((n, share + STAT, cols), BF16),
             pltpu.VMEM((n, share + STAT, cols), BF16),
-            pltpu.VMEM((rows, share), F32),
-            pltpu.VMEM((rows, value_width), F32),
             pltpu.VMEM((n, vshare, rows), BF16),
             pltpu.VMEM((n, vshare, rows), BF16),
-            pltpu.VMEM((2 * n * pad, 128), F32),
+            pltpu.VMEM((n * pad, 128), F32),
             pltpu.VMEM((2, n, pad, 128), BF16),
             pltpu.VMEM((2, n, pad, 128), BF16),
             dma((6,)),
             dma((2, half)), dma((2, half)),
-            dma((4,)), dma((4,)),
+            dma((PIECES + 1,)), dma((PIECES + 1,)),
+            dma((PIECES + 1,)), dma((PIECES + 1,)),
             dma((n,)), dma((n,)),
             dma((n,)), dma((n,)),
             dma((2, n)), dma((2, n)),
@@ -254,7 +266,7 @@
         compiler_params=pltpu.CompilerParams(
             collective_id=0, has_side_effects=True, vmem_limit_bytes=56 * 2**20
         ),
-    )(query_latent, query_rope, cache_latent, cache_rope, value_up, out_proj.reshape(wide, width))
+    )(query_latent, query_rope, cache_latent, cache_rope.T, value_up, out_proj.reshape(wide, width))
 
 
 def per_device(query_latent, query_rope, cache_latent, cache_rope, value_up, out_proj):

time: 33.9 us -> 31.3 us (0.923)
  local copies, waits for them, and re-layouts: 2.81 us -> 1.33 us
  Pallas kernels: 30.9 us -> 29.8 us
    unnamed x2 -> x1, local copies, waits for them, and re-layouts: 2.81 us -> 1.33 us
    pallas_call x1, Pallas kernels: 30.9 us -> 29.8 us  [fused(): pl.pallas_call(functools.partial(kernel, n), out_shape=jax.ShapeDtypeStru...]
where the time goes in v2:
time: 31.3 us; the launch traced here: 31.1 us
  Pallas kernels  29.8 us (95%)
  local copies, waits for them, and re-layouts  1.33 us (4%)
    pallas_call x1, Pallas kernels, fused(): pl.pallas_call(functools.partial(kernel, n), out_shape=jax.ShapeDtypeStru...  29.8 us
    unnamed x1, local copies, waits for them, and re-layouts  1.33 us

profile of v2, /device:TPU:0, one launch (start us, length us, event | category | flops | bytes accessed | tf_op | source)
XLA Modules:
  0.0 31.1 jit_solution(15747532262449964261)
XLA Ops:
  0.0 29.8 %shard_map.64 = bf16[1,3584]{1,0:T(2,128)(2,1)} custom-call(bf16[1,32,512]{2,1,0:T(8,128)(2,1)} %ql.1, bf16[1,32,64]{2,1,0:T(8,128)(2,1)} %qr.1, bf16[256,512]{1,0:T(8,128)(2,1)} %cl.1, bf16[64,256]{1,0:T(8,128)(2,1)} %bitcast.3, bf16[32,64,128]{2,1,0:T(8,128)(2,1)} %vu.1, bf16[512,7168]{1,0:T(8,128)(2,1)} %bitcast.2), custom_call_target="tpu_custom_call" | custom-call | tf_op jit(solution)/shard_map/pallas_call | solution.py:237
  29.8 1.3 %copy.8 = bf16[1,3584]{1,0:T(2,128)(2,1)} copy(bf16[1,3584]{1,0:T(2,128)(2,1)} %shard_map.64) | data formatting | bytes 14336

commit v3 on v2

--- a/solution.py
+++ b/solution.py
@@ -17,12 +17,16 @@
 STAT = 16
 
 
+def mod(a, b):
+    return a & (b - 1) if b & (b - 1) == 0 else a % b
+
+
+def div(a, b):
+    return a >> (b.bit_length() - 1) if b & (b - 1) == 0 else a // b
+
+
 def contract(a, b, da, db):
     return lax.dot_general(a, b, (((da,), (db,)), ((), ())), preferred_element_type=F32)
-
-
-def far_first(n):
-    return sorted(range(1, n), key=lambda d: abs(d - n // 2))
 
 
 def kernel(
@@ -59,7 +63,7 @@
         copy.start()
 
     barrier = pltpu.get_barrier_semaphore()
-    line = [2 * ((z + d) % half) + x for d in far_first(half)]
+    line = [2 * ((z + d) % half) + x for d in range(1, half)]
     for peer in line:
         pl.semaphore_signal(barrier, inc=1, device_id={"ctx": peer}, device_id_type=MESH)
     pl.semaphore_signal(barrier, inc=1, device_id={"ctx": partner}, device_id_type=MESH)
@@ -132,9 +136,9 @@
         lat_send[j, 0:share, :] = latent[j * share : (j + 1) * share].astype(BF16)
         lat_send[j, share : share + STAT, :] = stats
 
-    def exchange(send, recv, send_sem, recv_sem):
+    def exchange(send, recv, send_sem, recv_sem, earlier):
         copies = []
-        for d in far_first(n):
+        for d in range(1, n):
             peer = (me + d) % n
             copy = pltpu.make_async_remote_copy(
                 send.at[peer], recv.at[me], send_sem.at[d], recv_sem.at[d],
@@ -143,11 +147,13 @@
             copy.start()
             copies.append(copy)
         recv[me] = send[me]
+        for copy in earlier:
+            copy.wait_send()
         for copy in copies:
             copy.wait_recv()
         return copies
 
-    lat_copies = exchange(lat_send, lat_recv, l_send, l_recv)
+    lat_copies = exchange(lat_send, lat_recv, l_send, l_recv, queries + cache + swap)
 
     sides = []
     for side in range(2):
@@ -161,35 +167,36 @@
 
     per = max(256 // share, 1)
     stacked = jnp.concatenate([comb] * per, axis=0)
-    lane = lax.broadcasted_iota(jnp.int32, stacked.shape, 1) % heads
-    block = lax.broadcasted_iota(jnp.int32, stacked.shape, 0) // share
+    lane = mod(lax.broadcasted_iota(jnp.int32, stacked.shape, 1), heads)
+    block = div(lax.broadcasted_iota(jnp.int32, stacked.shape, 0), share)
+    ahead = lane - block
     flipped = jnp.zeros((vut.shape[0], rows), F32)
     for g in range(heads // per):
-        rhs = jnp.where(lane == block + g * per, stacked, 0.0).astype(BF16)
+        rhs = jnp.where(ahead == g * per, stacked, 0.0).astype(BF16)
         flipped += jnp.dot(
             vut[:, g * per * share : (g + 1) * per * share], rhs, preferred_element_type=F32
         )
     for j in range(n):
         pr_send[j] = flipped[j * vshare : (j + 1) * vshare].astype(BF16)
-    pr_copies = exchange(pr_send, pr_recv, p_send, p_recv)
+    pr_copies = exchange(pr_send, pr_recv, p_send, p_recv, lat_copies)
 
     head_out = sum(pr_recv[s].astype(F32) for s in range(n)).astype(BF16)
     wide = vshare * heads
     spread = (
-        lax.broadcasted_iota(jnp.int32, (vshare, wide), 1) // heads
+        div(lax.broadcasted_iota(jnp.int32, (vshare, wide), 1), heads)
         == lax.broadcasted_iota(jnp.int32, (vshare, wide), 0)
     ).astype(F32).astype(BF16)
     copied = contract(head_out, spread, 0, 0)
-    keep = (
-        lax.broadcasted_iota(jnp.int32, (rows, wide), 1) % heads
-        == lax.broadcasted_iota(jnp.int32, (rows, wide), 0) % heads
-    )
+    apart = lax.broadcasted_iota(jnp.int32, (rows, wide), 1) - lax.broadcasted_iota(
+        jnp.int32, (rows, wide), 0
+    )
+    keep = mod(apart, heads) == 0
     lhs = jnp.sum(jnp.where(keep, copied, 0.0).reshape(n, heads, wide), axis=1).astype(BF16)
 
     local[5].wait()
     step = 256 if chunks % 2 == 0 else 128
     at_copies = []
-    for e in (1, 0):
+    for e in (0, 1):
         other = (hd + e) % 2
         for c in range(chunks * 128 // step):
             at = pl.multiple_of(other * chunks * 128 + c * step, 128)
@@ -201,7 +208,7 @@
         for j in range(n):
             slot = (j % 2) * half + j // 2
             at_send[other, j] = att[slot * pad : (slot + 1) * pad, :].astype(BF16)
-        for d in far_first(n) + [0] * e:
+        for d in [*range(1, n)] + [0] * e:
             peer = (me + d) % n
             copy = pltpu.make_async_remote_copy(
                 at_send.at[other, peer], at_recv.at[hd, me], a_send.at[e, d], a_recv.at[e, d],
@@ -210,13 +217,15 @@
             copy.start()
             at_copies.append(copy)
     at_recv[hd, me] = at_send[hd, me]
+    for copy in pr_copies:
+        copy.wait_send()
     for copy in at_copies:
         copy.wait_recv()
     result = sum(at_recv[k, s].astype(F32) for k in range(2) for s in range(n)).astype(BF16)
     for c in range(chunks):
         out[0:1, c * 128 : (c + 1) * 128] = result[c : c + 1, :]
 
-    for copy in cache + queries + swap + lat_copies + pr_copies + at_copies:
+    for copy in at_copies:
         copy.wait_send()
 
 

time: 31.3 us -> 29.3 us (0.936)
  Pallas kernels: 29.8 us -> 27.8 us
    pallas_call x1, Pallas kernels: 29.8 us -> 27.8 us  [fused(): pl.pallas_call(functools.partial(kernel, n), out_shape=jax.ShapeDtypeStru...]
where the time goes in v3:
time: 29.3 us; the launch traced here: 29.1 us
  Pallas kernels  27.8 us (95%)
  local copies, waits for them, and re-layouts  1.33 us (5%)
    pallas_call x1, Pallas kernels, fused(): pl.pallas_call(functools.partial(kernel, n), out_shape=jax.ShapeDtypeStru...  27.8 us
    unnamed x1, local copies, waits for them, and re-layouts  1.33 us

profile of v3, /device:TPU:0, one launch (start us, length us, event | category | flops | bytes accessed | tf_op | source)
XLA Modules:
  0.0 29.1 jit_solution(18016099668187886219)
XLA Ops:
  0.0 27.8 %shard_map.64 = bf16[1,3584]{1,0:T(2,128)(2,1)} custom-call(bf16[1,32,512]{2,1,0:T(8,128)(2,1)} %ql.1, bf16[1,32,64]{2,1,0:T(8,128)(2,1)} %qr.1, bf16[256,512]{1,0:T(8,128)(2,1)} %cl.1, bf16[64,256]{1,0:T(8,128)(2,1)} %bitcast.3, bf16[32,64,128]{2,1,0:T(8,128)(2,1)} %vu.1, bf16[512,7168]{1,0:T(8,128)(2,1)} %bitcast.2), custom_call_target="tpu_custom_call" | custom-call | tf_op jit(solution)/shard_map/pallas_call | solution.py:246
  27.8 1.3 %copy.8 = bf16[1,3584]{1,0:T(2,128)(2,1)} copy(bf16[1,3584]{1,0:T(2,128)(2,1)} %shard_map.64) | data formatting | bytes 14336

commit v4 on v3

--- a/solution.py
+++ b/solution.py
@@ -38,8 +38,8 @@
     me = lax.axis_index("ctx")
     hd = lax.axis_index("head")
     half = n // 2
-    z = me // 2
-    x = me % 2
+    z = div(me, 2)
+    x = mod(me, 2)
     partner = 2 * z + 1 - x
     heads = ql.shape[1]
     tokens = cl.shape[0]
@@ -59,11 +59,11 @@
         pltpu.make_async_copy(vu, vub, local_sem.at[4]),
         pltpu.make_async_copy(wo, wob, local_sem.at[5]),
     ]
-    for copy in local:
+    for copy in local[:5]:
         copy.start()
 
     barrier = pltpu.get_barrier_semaphore()
-    line = [2 * ((z + d) % half) + x for d in range(1, half)]
+    line = [2 * mod(z + d, half) + x for d in range(1, half)]
     for peer in line:
         pl.semaphore_signal(barrier, inc=1, device_id={"ctx": peer}, device_id_type=MESH)
     pl.semaphore_signal(barrier, inc=1, device_id={"ctx": partner}, device_id_type=MESH)
@@ -94,7 +94,7 @@
                     device_id={"ctx": peer}, device_id_type=MESH,
                 )
             )
-    for copy in queries + cache:
+    for copy in queries + cache + local[5:]:
         copy.start()
 
     for copy in local[:5]:
@@ -138,8 +138,8 @@
 
     def exchange(send, recv, send_sem, recv_sem, earlier):
         copies = []
-        for d in range(1, n):
-            peer = (me + d) % n
+        for d in [*range(1, n, 2), *range(2, n, 2)]:
+            peer = mod(me + d, n)
             copy = pltpu.make_async_remote_copy(
                 send.at[peer], recv.at[me], send_sem.at[d], recv_sem.at[d],
                 device_id={"ctx": peer}, device_id_type=MESH,
@@ -166,13 +166,13 @@
     comb = jnp.concatenate(sides, axis=1)
 
     per = max(256 // share, 1)
-    stacked = jnp.concatenate([comb] * per, axis=0)
+    stacked = jnp.concatenate([comb.astype(BF16)] * per, axis=0)
     lane = mod(lax.broadcasted_iota(jnp.int32, stacked.shape, 1), heads)
     block = div(lax.broadcasted_iota(jnp.int32, stacked.shape, 0), share)
     ahead = lane - block
     flipped = jnp.zeros((vut.shape[0], rows), F32)
     for g in range(heads // per):
-        rhs = jnp.where(ahead == g * per, stacked, 0.0).astype(BF16)
+        rhs = jnp.where(ahead == g * per, stacked, jnp.zeros((), BF16))
         flipped += jnp.dot(
             vut[:, g * per * share : (g + 1) * per * share], rhs, preferred_element_type=F32
         )
@@ -197,7 +197,7 @@
     step = 256 if chunks % 2 == 0 else 128
     at_copies = []
     for e in (0, 1):
-        other = (hd + e) % 2
+        other = mod(hd + e, 2)
         for c in range(chunks * 128 // step):
             at = pl.multiple_of(other * chunks * 128 + c * step, 128)
             value = jnp.dot(lhs, wob[:, pl.ds(at, step)], preferred_element_type=F32)
@@ -209,7 +209,7 @@
             slot = (j % 2) * half + j // 2
             at_send[other, j] = att[slot * pad : (slot + 1) * pad, :].astype(BF16)
         for d in [*range(1, n)] + [0] * e:
-            peer = (me + d) % n
+            peer = mod(me + d, n)
             copy = pltpu.make_async_remote_copy(
                 at_send.at[other, peer], at_recv.at[hd, me], a_send.at[e, d], a_recv.at[e, d],
                 device_id={"ctx": peer, "head": other}, device_id_type=MESH,

time: 29.3 us -> 29.2 us (level)
  no operation moved by 1% of the time
where the time goes in v4:
time: 29.2 us; the launch traced here: 28.9 us
  Pallas kernels  27.6 us (95%)
  local copies, waits for them, and re-layouts  1.33 us (5%)
    pallas_call x1, Pallas kernels, fused(): pl.pallas_call(functools.partial(kernel, n), out_shape=jax.ShapeDtypeStru...  27.6 us
    unnamed x1, local copies, waits for them, and re-layouts  1.33 us

profile of v4, /device:TPU:0, one launch (start us, length us, event | category | flops | bytes accessed | tf_op | source)
XLA Modules:
  0.0 28.9 jit_solution(14730794313097336873)
XLA Ops:
  0.0 27.6 %shard_map.64 = bf16[1,3584]{1,0:T(2,128)(2,1)} custom-call(bf16[1,32,512]{2,1,0:T(8,128)(2,1)} %ql.1, bf16[1,32,64]{2,1,0:T(8,128)(2,1)} %qr.1, bf16[256,512]{1,0:T(8,128)(2,1)} %cl.1, bf16[64,256]{1,0:T(8,128)(2,1)} %bitcast.3, bf16[32,64,128]{2,1,0:T(8,128)(2,1)} %vu.1, bf16[512,7168]{1,0:T(8,128)(2,1)} %bitcast.2), custom_call_target="tpu_custom_call" | custom-call | tf_op jit(solution)/shard_map/pallas_call | solution.py:246
  27.6 1.3 %copy.8 = bf16[1,3584]{1,0:T(2,128)(2,1)} copy(bf16[1,3584]{1,0:T(2,128)(2,1)} %shard_map.64) | data formatting | bytes 14336
